TPU v7x, 32 devices: a whole 2x2x4 slice. The times are simulated.
32 devices in a mesh: ao: 4 (over y, x), prow: 4 (over z), pcol: 2 (over core).
Axes of the slice: x: 2, y: 2, z: 4, core: 2. Of those that a mesh axis runs over, the one named last changes fastest.
Arguments:
- three_index: bfloat16 [512, 1200, 1200], P(('prow', 'pcol'), 'ao'), may hold values from -1.2578125 to 1.2578125
- coefficients: bfloat16 [1200, 120], replicated, may hold values from -0.1875 to 0.1875
Outputs:
- coulomb: bfloat16 [14400, 14400], P('ao', ('prow', 'pcol'))
All inputs are finite; a program needn't handle non-finite values.
Results may differ from a plain program's by a relative error of at most 0.0069.
Values may be sent and summed in bfloat16 or wider, within the bound.
A program may use at most 256 MiB of HBM per device.

v0:
```python
import jax
import jax.numpy as jnp
from jax import lax
from jax.sharding import PartitionSpec as P


def on_device(three_index, coefficients):
    aux_local, rows_local, basis = three_index.shape
    active = coefficients.shape[1]
    pair_count = active * active
    half = jnp.dot(
        three_index.reshape(aux_local * rows_local, basis),
        coefficients,
        preferred_element_type=jnp.float32,
    )
    half = half.astype(jnp.bfloat16).reshape(aux_local, rows_local, active)
    local_rows = lax.dynamic_slice_in_dim(
        coefficients, lax.axis_index("ao") * rows_local, rows_local, 0
    )
    partial_ints = jnp.einsum("mp,amq->apq", local_rows, half, preferred_element_type=jnp.float32)
    partial_ints = partial_ints.reshape(aux_local, pair_count)
    row_width = pair_count // lax.axis_size("ao")
    summed = lax.psum(partial_ints, "ao").astype(jnp.bfloat16)
    own_rows = lax.dynamic_slice_in_dim(summed, lax.axis_index("ao") * row_width, row_width, 1)
    column_panel = lax.all_to_all(summed, ("prow", "pcol"), split_axis=1, concat_axis=0, tiled=True)
    coulomb = lax.dot_general(
        lax.all_gather(own_rows, ("prow", "pcol"), axis=0, tiled=True),
        column_panel,
        (((0,), (0,)), ((), ())),
        preferred_element_type=jnp.float32,
    )
    return coulomb.astype(jnp.bfloat16)


def solution(mesh):
    placed = (P(("prow", "pcol"), "ao", None), P())
    return jax.shard_map(
        on_device, mesh=mesh, in_specs=placed, out_specs=P("ao", ("prow", "pcol")), check_vma=False
    )
```

profile of v0, /device:TPU:4, one launch (start us, length us, event | category | flops | bytes accessed | tf_op | source)
XLA Modules:
  0.0 386.2 jit_solution(10995936429763283574)
XLA Ops:
  6.5 0.0 copy-start
  6.5 0.0 all-gather.2.cloned.1.call-start
  6.5 33.7 %copy.4 = bf16[64,300,1200]{2,1,0:T(8,128)(2,1)} copy(bf16[64,300,1200]{2,0,1:T(8,128)(2,1)} %param.2) | data formatting | bytes 92160000 | tf_op args[0]
  40.2 51.4 %reshape.12 = bf16[19200,1200]{1,0:T(8,128)(2,1)} reshape(bf16[64,300,1200]{2,1,0:T(8,128)(2,1)} %copy.4) | data formatting | bytes 92160000 | tf_op jit(solution)/shard_map/reshape | solution.py:12
  91.6 0.0 copy-done
  91.6 24.0 %convolution_convert_fusion = bf16[19200,120]{0,1:T(8,128)(2,1)} fusion(bf16[19200,1200]{1,0:T(8,128)(2,1)} %reshape.12, bf16[1200,120]{1,0:T(8,128)(2,1)S(1)} %copy-done), kind=kOutput, calls=%fused_computation | convolution fusion | flops 5531904000 | bytes 50976000 | tf_op jit(solution)/shard_map/dot_general | solution.py:11
  115.5 15.6 %reshape.16 = bf16[64,300,120]{1,0,2:T(8,128)(2,1)} reshape(bf16[19200,120]{0,1:T(8,128)(2,1)} %convolution_convert_fusion) | data formatting | bytes 9216000 | tf_op jit(solution)/shard_map/reshape | solution.py:16
  131.2 11.5 %fusion.2 = f32[64,120,120]{1,2,0:T(8,128)} fusion(bf16[64,300,120]{1,0,2:T(8,128)(2,1)} %reshape.16, bf16[1200,120]{1,0:T(8,128)(2,1)S(1)} %copy-done, s32[]{:T(128)S(6)} %select_n.6), kind=kOutput, calls=%fused_computation.4 | convolution fusion | flops 552960000 | bytes 8372228 | tf_op jit(solution)/shard_map/mp,amq->apq/dot_general | solution.py:20
  142.6 5.4 %copy.6 = f32[64,120,120]{2,1,0:T(8,128)} copy(f32[64,120,120]{1,2,0:T(8,128)} %fusion.2) | data formatting | bytes 7372800 | tf_op jit(solution)/shard_map/mp,amq->apq/transpose | solution.py:20
  148.0 5.0 %reshape.14 = f32[64,14400]{1,0:T(8,128)} reshape(f32[64,120,120]{2,1,0:T(8,128)} %copy.6) | data formatting | bytes 7372800 | tf_op jit(solution)/shard_map/reshape | solution.py:21
  153.0 128.2 %all-reduce.1 = bf16[64,14400]{1,0:T(8,128)(2,1)S(1)} all-reduce(f32[64,14400]{1,0:T(8,128)} %reshape.14), channel_id=1, replica_groups=mesh['ao'=4,'prow'=4,'pcol'=2] {'ao'}, use_global_device_ids=true, to_apply=%region_0.0 | all-reduce | flops 921600 | bytes 5529600 | tf_op jit(solution)/shard_map/psum | solution.py:23
  281.3 1.0 constant_dynamic-slice_fusion
  282.2 0.0 all-gather.2.cloned.1.call-update
  282.3 3.6 all_to_all.14
  285.8 1.8 copy.7
  287.7 79.3 %all_to_all.19 = bf16[64,8,1800]{2,0,1:T(8,128)(2,1)S(1)} all-to-all(bf16[64,8,1800]{2,0,1:T(8,128)(2,1)S(1)} %copy.7), channel_id=1, replica_groups=mesh['ao'=4,'prow'=4,'pcol'=2] {'prow','pcol'}, dimensions={1} | all-to-all | bytes 3686400 | tf_op jit(solution)/shard_map/all_to_all | solution.py:25
  367.0 0.0 all-gather.2.cloned.1.call-done
  367.0 12.3 %convolution_convert_fusion.1 = bf16[3600,1800]{0,1:T(8,128)(2,1)} fusion(bf16[512,3600]{1,0:T(8,128)(2,1)} %all-gather.2.cloned.1.call-done, bf16[512,1800]{1,0:T(8,128)(2,1)S(1)} %bitcast.14), kind=kOutput, calls=%fused_computation.1 | convolution fusion | flops 6641999872 | bytes 18489600 | tf_op jit(solution)/shard_map/dot_general | solution.py:26
Async XLA Ops:
  6.5 85.0 %copy-start = (bf16[1200,120]{1,0:T(8,128)(2,1)S(1)}, bf16[1200,120]{1,0:T(8,128)(2,1)}, u32[]{:S(2)}) copy-start(bf16[1200,120]{1,0:T(8,128)(2,1)} %param.3) | copy-start | bytes 864004
  6.5 360.5 %all-gather.2.cloned.1.call-start = ((), (), s32[]{:S(2)}) async-start(), calls=%async_computation.1 | async-start | bytes 4276224 | tf_op jit(solution)/shard_map/all_gather | solution.py:27
Sparse Core Ops, SparseCore 0:
  282.4 79.5 all-gather.1
where the time goes:
time: 389 us; the launch traced here: 386 us
  blocking collectives  208 us (53%)
  local copies, waits for them, and re-layouts  117 us (30%)
  matrix products  47.7 us (12%)
  between operations  13.4 us (3%)
    psum x1, blocking collectives, on_device(): summed = lax.psum(partial_ints, 'ao').astype(jnp.bfloat16)  128 us
    all_to_all x1, blocking collectives, on_device(): lax.all_to_all(summed, ('prow', 'pcol'), split_axis=1, concat_axis=0, til...  79.3 us
    reshape x1, local copies, waits for them, and re-layouts, on_device(): three_index.reshape(aux_local * rows_local, basis)  51.4 us
    unnamed x3, local copies, waits for them, and re-layouts  33.7 us
    dot_general x1, matrix products, on_device(): jnp.dot(three_index.reshape(aux_local * rows_local, basis), coefficients,...  24 us
    reshape x1, local copies, waits for them, and re-layouts, on_device(): half = half.astype(jnp.bfloat16).reshape(aux_local, rows_local, active)  15.6 us
    dot_general x1, matrix products, on_device(): lax.dot_general(lax.all_gather(own_rows, ('prow', 'pcol'), axis=0, tiled=...  12.3 us
    dot_general x1, matrix products, on_device(): jnp.einsum('mp,amq->apq', local_rows, half, preferred_element_type=jnp.fl...  11.5 us
  transfers between devices with their start and end apart: 1, of which 0 were waited for; matrix products, arithmetic and copies ran while one was open for 0% of the time, Pallas kernels for 0%

commit v1 on v0

v1 whole, which is shorter than its diff:
```python
import functools

import jax
import jax.numpy as jnp
from jax import lax
from jax.experimental import pallas as pl
from jax.experimental.pallas import tpu as pltpu
from jax.sharding import PartitionSpec as P

CHUNK = 16
SLOTS = 4
MESH = pl.DeviceIdType.MESH


def rounded(size, unit):
    return -(-size // unit) * unit


def kernel(
    dims, three_ref, coef_ref, rows_ref, x_out, y_out,
    ring, halves, part, sending, arrived, own, pack, x, y,
    ring_sem, rs_send, rs_recv, ag_send, ag_recv, sib_send, sib_recv, y_send, y_recv, out_sem,
):
    nao, nrow, ncol, chunks, active, width, panels = dims
    ao, row, col = lax.axis_index("ao"), lax.axis_index("prow"), lax.axis_index("pcol")
    groups = nrow * ncol
    block = active // nao
    block_rows = block * CHUNK
    batch = ring.shape[1]
    basis_rows = three_ref.shape[0]
    steps = basis_rows // batch
    total_steps = chunks * steps

    def load(step, slot):
        return pltpu.make_async_copy(
            three_ref.at[
                pl.ds(lax.rem(step, steps) * batch, batch),
                pl.ds(pl.multiple_of(lax.div(step, steps) * CHUNK, CHUNK), CHUNK),
            ],
            ring.at[slot],
            ring_sem.at[slot],
        )

    for slot in range(SLOTS):
        load(slot, slot).start()

    barrier = pltpu.get_barrier_semaphore()
    partners = [{"ao": lax.rem(ao + d, nao)} for d in range(1, nao)]
    partners += [{"pcol": lax.rem(col + d, ncol)} for d in range(1, ncol)]
    partners += [{"prow": lax.rem(row + d, nrow)} for d in range(1, nrow)]
    for partner in partners:
        pl.semaphore_signal(barrier, inc=1, device_id=partner, device_id_type=MESH)
    pl.semaphore_wait(barrier, len(partners))

    pack[...] = jnp.zeros_like(pack)

    def remote(src, dst, send, recv, where):
        return pltpu.make_async_remote_copy(
            src_ref=src, dst_ref=dst, send_sem=send, recv_sem=recv,
            device_id=where, device_id_type=MESH,
        )

    def panel_rows(j, at_row, at_col):
        start = (j * groups + at_row * ncol + at_col) * CHUNK
        return pl.ds(pl.multiple_of(start, CHUNK), CHUNK)

    def pair_rows(j, at_row):
        start = (j * groups + at_row * ncol) * CHUNK
        return pl.ds(pl.multiple_of(start, CHUNK), ncol * CHUNK)

    def rs_copy(j, d):
        target = lax.rem(ao + d, nao)
        src = sending.at[j, pl.ds(pl.multiple_of(target * block_rows, CHUNK), block_rows)]
        return remote(
            src, arrived.at[j, d - 1], rs_send.at[j, d - 1], rs_recv.at[j, d - 1], {"ao": target}
        )

    def ag_copy(j, origin, hop, direction):
        at = x.at[panel_rows(j, origin, col)]
        where = {"prow": row + 1 if direction == 0 else row - 1}
        return remote(at, at, ag_send.at[j, hop, direction], ag_recv.at[j, hop, direction], where)

    def sib_copy(j, origin, slot, d):
        at = x.at[panel_rows(j, origin, col)]
        where = {"pcol": lax.rem(col + d, ncol)}
        return remote(at, at, sib_send.at[j, slot, d - 1], sib_recv.at[j, slot, d - 1], where)

    def sib_arrival(j, origin, slot, d):
        source = lax.rem(col + ncol - d, ncol)
        at = x.at[panel_rows(j, origin, source)]
        where = {"pcol": lax.rem(col + d, ncol)}
        return remote(at, at, sib_send.at[j, slot, d - 1], sib_recv.at[j, slot, d - 1], where)

    def ring_place(index):
        half = lax.div(index, 2)
        return jnp.where(lax.rem(index, 2) == 0, half, nao - 1 - half)

    def ring_index(place):
        return jnp.where(place < nao // 2, 2 * place, 2 * (nao - 1 - place) + 1)

    place, owner = ring_place(ao), ring_place(row)
    away = (lax.rem(place - owner + nao, nao), lax.rem(owner - place + nao, nao))
    onward = (
        ring_index(lax.rem(place + 1, nao)),
        ring_index(lax.rem(place + nao - 1, nao)),
    )

    def y_copy(j, origin, slot, way):
        at = y.at[pair_rows(j, origin)]
        return remote(at, at, y_send.at[j, slot], y_recv.at[j, slot], {"ao": onward[way]})

    def cut(j, origin):
        rows = pair_rows(j, origin)
        for h in range(panels):
            @pl.when(col == h)
            def _():
                low = h * width
                base = low // 128 * 128
                stop = rounded(low + width, 128)
                wide = x[rows, base:stop].astype(jnp.float32)
                piece = wide[:, low - base:low - base + width]
                y[rows, :width] = piece.astype(jnp.bfloat16)

    places = [(0, 0, 0, row, row >= 0)]
    for hop in range(1, nrow):
        places.append((2 * hop - 1, hop, 0, row - hop, row - hop >= 0))
        places.append((2 * hop, hop, 1, row + hop, row + hop < nrow))

    def compute(j):
        def body(i, carry):
            step = j * steps + i
            slot = lax.rem(step, SLOTS)
            load(step, slot).wait()
            rows = ring[slot].reshape(batch * CHUNK, ring.shape[3])
            start = pl.multiple_of(i * (batch * CHUNK), CHUNK)
            halves[pl.ds(start, batch * CHUNK), :] = jnp.dot(
                rows, coef_ref[...], preferred_element_type=jnp.float32
            )

            @pl.when(step + SLOTS < total_steps)
            def _():
                load(step + SLOTS, slot).start()

            return carry

        lax.fori_loop(0, steps, body, 0)
        for u in range(CHUNK):
            half = halves[pl.ds(u, basis_rows, stride=CHUNK), :].astype(jnp.bfloat16)
            part[pl.ds(u, active, stride=CHUNK), :] = jnp.dot(
                rows_ref[...], half, preferred_element_type=jnp.float32
            )
        sending[j] = part[...].astype(jnp.bfloat16)
        own[j] = part[pl.ds(pl.multiple_of(ao * block_rows, CHUNK), block_rows), :]
        for d in range(1, nao):
            rs_copy(j, d).start()

    def combine(j):
        for d in range(1, nao):
            rs_copy(j, d).wait_recv()
        for p in range(block):
            rows = pl.ds(p * CHUNK, CHUNK)
            value = own[j, rows, :]
            for d in range(1, nao):
                value = value + arrived[j, d - 1, rows, :].astype(jnp.float32)
            first = p * active
            pack[:, first:first + active] = value[:, :active]
        x[panel_rows(j, row, col), :] = pack[...].astype(jnp.bfloat16)

        @pl.when(row < nrow - 1)
        def _():
            ag_copy(j, row, 1, 0).start()

        @pl.when(row > 0)
        def _():
            ag_copy(j, row, 1, 1).start()

        for d in range(1, ncol):
            sib_copy(j, row, 0, d).start()

    def onward_on_line(direction):
        return row < nrow - 1 if direction == 0 else row > 0

    def in_chunks(j):
        return jnp.logical_and(j >= 0, j < chunks)

    def tick(t, carry):
        @pl.when(t < chunks)
        def _():
            compute(t)

        @pl.when(in_chunks(t - 1))
        def _():
            combine(t - 1)

        for slot, hop, direction, origin, there in places:
            if hop == 0:
                continue
            j = t - 1 - hop

            @pl.when(jnp.logical_and(in_chunks(j), there))
            def _():
                ag_copy(j, origin, hop, direction).wait_recv()
                if hop < nrow - 1:
                    @pl.when(onward_on_line(direction))
                    def _():
                        ag_copy(j, origin, hop + 1, direction).start()
                for d in range(1, ncol):
                    sib_copy(j, origin, slot, d).start()

        for slot, hop, direction, origin, there in places:
            j = t - 2 - hop

            @pl.when(jnp.logical_and(in_chunks(j), there))
            def _():
                for d in range(1, ncol):
                    sib_arrival(j, origin, slot, d).wait_recv()

            for way in range(2):
                k = t - 2 - hop - away[way]
                mine = lax.rem(k + slot + 2 * chunks * nrow * nao, 2) == way

                @pl.when(jnp.logical_and(jnp.logical_and(in_chunks(k), there), mine))
                def _():
                    @pl.when(away[way] == 0)
                    def _():
                        cut(k, origin)
                        y_copy(k, origin, slot, way).start()

                    @pl.when(away[way] > 0)
                    def _():
                        y_copy(k, origin, slot, way).wait_recv()

                        @pl.when(away[way] < nao - 1)
                        def _():
                            y_copy(k, origin, slot, way).start()

        return carry

    lax.fori_loop(0, chunks + nrow + nao, tick, 0)

    x_copy = pltpu.make_async_copy(x, x_out, out_sem.at[0])
    x_copy.start()

    y_finish = pltpu.make_async_copy(y, y_out, out_sem.at[1])
    y_finish.start()
    y_finish.wait()
    x_copy.wait()

    def drain(j, carry):
        for d in range(1, nao):
            rs_copy(j, d).wait_send()
        for slot, hop, direction, origin, there in places:
            @pl.when(there)
            def _():
                for d in range(1, ncol):
                    sib_copy(j, origin, slot, d).wait_send()
                if hop < nrow - 1:
                    for way in ((0, 1) if hop == 0 else (direction,)):
                        @pl.when(onward_on_line(way))
                        def _():
                            ag_copy(j, origin, hop + 1, way).wait_send()
                for way in range(2):
                    mine = lax.rem(j + slot, 2) == way

                    @pl.when(jnp.logical_and(mine, away[way] < nao - 1))
                    def _():
                        y_copy(j, origin, slot, way).wait_send()

        return carry

    lax.fori_loop(0, chunks, drain, 0)


def on_device(sizes, three_index, coefficients):
    nao, nrow, ncol = sizes
    aux_local, rows_local, basis = three_index.shape
    active = coefficients.shape[1]
    pairs = active * active
    groups = nrow * ncol
    assert nao == nrow and groups % nao == 0 and groups // nao == ncol
    assert active % nao == 0 and aux_local % CHUNK == 0
    panels = ncol
    width = pairs // groups
    padded = rounded(width, 128)
    row_width = pairs // nao
    row_padded = rounded(row_width, 128)
    steps = max(s for s in range(1, 6) if rows_local % s == 0)
    lanes = rounded(active, 128)
    chunks = aux_local // CHUNK
    aux = aux_local * groups
    block_rows = active // nao * CHUNK
    local_rows = lax.dynamic_slice_in_dim(
        coefficients, lax.axis_index("ao") * rows_local, rows_local, 0
    ).T
    coefs = jnp.pad(coefficients, ((0, 0), (0, lanes - active)))
    dma = pltpu.SemaphoreType.DMA
    dims = (nao, nrow, ncol, chunks, active, width, panels)
    x, y = pl.pallas_call(
        functools.partial(kernel, dims),
        out_shape=(
            jax.ShapeDtypeStruct((aux, row_padded), jnp.bfloat16),
            jax.ShapeDtypeStruct((aux, padded), jnp.bfloat16),
        ),
        in_specs=[
            pl.BlockSpec(memory_space=pl.ANY),
            pl.BlockSpec(memory_space=pltpu.VMEM),
            pl.BlockSpec(memory_space=pltpu.VMEM),
        ],
        out_specs=(pl.BlockSpec(memory_space=pl.ANY), pl.BlockSpec(memory_space=pl.ANY)),
        scratch_shapes=[
            pltpu.VMEM((SLOTS, rows_local // steps, CHUNK, basis), jnp.bfloat16),
            pltpu.VMEM((rows_local * CHUNK, lanes), jnp.float32),
            pltpu.VMEM((active * CHUNK, lanes), jnp.float32),
            pltpu.VMEM((chunks, active * CHUNK, lanes), jnp.bfloat16),
            pltpu.VMEM((chunks, nao - 1, block_rows, lanes), jnp.bfloat16),
            pltpu.VMEM((chunks, block_rows, lanes), jnp.float32),
            pltpu.VMEM((CHUNK, row_padded), jnp.float32),
            pltpu.VMEM((aux, row_padded), jnp.bfloat16),
            pltpu.VMEM((aux, padded), jnp.bfloat16),
            dma((SLOTS,)),
            dma((chunks, nao - 1)),
            dma((chunks, nao - 1)),
            dma((chunks, nrow, 2)),
            dma((chunks, nrow, 2)),
            dma((chunks, 2 * nrow - 1, ncol - 1)),
            dma((chunks, 2 * nrow - 1, ncol - 1)),
            dma((chunks, 2 * nrow - 1)),
            dma((chunks, 2 * nrow - 1)),
            dma((2,)),
        ],
        compiler_params=pltpu.CompilerParams(
            collective_id=0, has_side_effects=True, vmem_limit_bytes=44 * 2**20
        ),
    )(jnp.transpose(three_index, (1, 0, 2)), coefs, local_rows)
    mirrored = lax.dot_general(
        y[:, :width], x[:, :row_width], (((0,), (0,)), ((), ())), preferred_element_type=jnp.float32
    )
    return mirrored.astype(jnp.bfloat16).T


def solution(mesh):
    sizes = tuple(mesh.shape[axis] for axis in ("ao", "prow", "pcol"))
    placed = (P(("prow", "pcol"), "ao", None), P())
    return jax.shard_map(
        functools.partial(on_device, sizes), mesh=mesh, in_specs=placed,
        out_specs=P("ao", ("prow", "pcol")), check_vma=False,
    )
```

time: 389 us -> 89.9 us (0.23)
  blocking collectives: 208 us -> 0 us
  local copies, waits for them, and re-layouts: 117 us -> 2.06 us
  Pallas kernels: 0 us -> 77.7 us
  matrix products: 47.7 us -> 9.93 us
  between operations: 13.4 us -> 0.02 us
    psum x1 -> x0, blocking collectives: 128 us -> none  [on_device(): summed = lax.psum(partial_ints, 'ao').astype(jnp.bfloat16)]
    all_to_all x1 -> x0, blocking collectives: 79.3 us -> none  [on_device(): lax.all_to_all(summed, ('prow', 'pcol'), split_axis=1, concat_axis=0, til...]
    pallas_call x0 -> x1, Pallas kernels: none -> 77.7 us  [on_device(): pl.pallas_call(functools.partial(kernel, dims), out_shape=(jax.ShapeDtype...]
    reshape x3 -> x0, local copies, waits for them, and re-layouts: 72 us -> none  [the longest x1 51.4 us: on_device(): three_index.reshape(aux_local * rows_local, basis)]
    dot_general x3 -> x1, matrix products: 47.7 us -> 9.93 us  [on_device(): lax.dot_general(y[:, :width], x[:, :row_width], (((0,), (0,)), ((), ())),...]
    unnamed x3 -> x1, local copies, waits for them, and re-layouts: 33.7 us -> 0.12 us
    all_to_all x2 -> x0, local copies, waits for them, and re-layouts: 5.4 us -> none  [on_device(): lax.all_to_all(summed, ('prow', 'pcol'), split_axis=1, concat_axis=0, til...]
    transpose x1 -> x0, local copies, waits for them, and re-layouts: 5.38 us -> none  [on_device(): jnp.einsum('mp,amq->apq', local_rows, half, preferred_element_type=jnp.fl...]
  transfers between devices with their start and end apart: 1 -> 0, of which waited for: 0 -> 0; matrix products, arithmetic and copies ran while one was open for 0% -> 0% of each run, Pallas kernels for 0% -> 0%
where the time goes in v1:
time: 89.9 us; the launch traced here: 89.7 us
  Pallas kernels  77.7 us (86%)
  matrix products  9.93 us (11%)
  local copies, waits for them, and re-layouts  2.06 us (2%)
    pallas_call x1, Pallas kernels, on_device(): pl.pallas_call(functools.partial(kernel, dims), out_shape=(jax.ShapeDtype...  77.7 us
    dot_general x1, matrix products, on_device(): lax.dot_general(y[:, :width], x[:, :row_width], (((0,), (0,)), ((), ())),...  9.93 us

profile of v1, /device:TPU:4, one launch (start us, length us, event | category | flops | bytes accessed | tf_op | source)
XLA Modules:
  0.0 89.7 jit_solution(8157541568202352523)
XLA Ops:
  0.0 0.9 %constant_dynamic-slice_fusion = bf16[300,120]{1,0:T(8,128)(2,1)S(1)} fusion(bf16[1200,120]{1,0:T(8,128)(2,1)} %param.3, s32[]{:T(128)S(6)} %select_n.3), kind=kLoop, calls=%fused_computation.3 | loop fusion | bytes 144004 | tf_op jit(solution)/shard_map/dynamic_slice | solution.py:292
  0.9 0.1 copy.4
  1.0 1.0 %pad.4.coef_ref = bf16[1200,128]{1,0:T(8,128)(2,1)S(1)} pad(bf16[1200,120]{1,0:T(8,128)(2,1)} %param.3, bf16[]{:T(256)} %constant.3.clone.1), padding=0_0x0_8 | pad | bytes 595202 | tf_op jit(solution)/shard_map/jit(_pad)/pad | solution.py:295
  2.1 77.7 %shard_map.28 = (bf16[512,3712]{1,0:T(8,128)(2,1)S(1)}, bf16[512,1920]{1,0:T(8,128)(2,1)S(1)}) custom-call(bf16[300,64,1200]{2,1,0:T(8,128)(2,1)} %bitcast.3, bf16[1200,128]{1,0:T(8,128)(2,1)S(1)} %pad.4.coef_ref, bf16[120,300]{1,0:T(8,128)(2,1)S(1)} %bitcast.2), custom_call_target="tpu_custom_call" | custom-call | tf_op jit(solution)/shard_map/pallas_call | solution.py:298
  79.8 9.9 %convolution_convert_fusion = bf16[3600,1800]{0,1:T(8,128)(2,1)} fusion(bf16[512,3712]{1,0:T(8,128)(2,1)S(1)} %get-tuple-element.7, bf16[512,1920]{1,0:T(8,128)(2,1)S(1)} %get-tuple-element.8), kind=kOutput, calls=%fused_computation | convolution fusion | flops 6641999872 | bytes 18727168 | tf_op jit(solution)/shard_map/dot_general | solution.py:335
